TPU v7x, 512 devices: a whole 4x8x8 slice. The times are simulated.
512 devices in a mesh: seq: 32 (over x, y_lo, core), ch: 16 (over y_hi, z).
Axes of the slice: x: 4, y: 8 (y_hi: 2, y_lo: 4; y = y_hi * 4 + y_lo), z: 8, core: 2. Of those that a mesh axis runs over, the one named last changes fastest.
Arguments:
- inputs: bfloat16 [4096, 4096], P('seq', 'ch'), may hold values from -6 to 6
- out_grad: bfloat16 [4096, 4096], P('seq', 'ch'), may hold values from -6 to 6
- embed_weight: float32 [32, 64], replicated, may hold values from -3 to 3
- filter_weight: float32 [64, 4096], P(None, 'ch'), may hold values from -0.01171875 to 0.01171875
- decay_rate: float32 [4096], P('ch'), may hold values from 0.1 to 128
- skip_gain: float32 [4096], P('ch'), may hold values from 0.5 to 1.5
Outputs:
- signal_grad: bfloat16 [4096, 4096], P('seq', 'ch')
- filter_grad: float32 [64, 4096], P(None, 'ch')
- embed_grad: float32 [32, 64], replicated
All inputs are finite; a program needn't handle non-finite values.
Results may differ from a plain program's by a relative error of at most 0.002.
Values may be sent and summed in bfloat16 or wider, within the bound.
A program may use at most 64 MiB of HBM per device.

v0:
```python
import functools
import math

import jax
import jax.numpy as jnp
import ml_dtypes
import numpy as np
from jax import lax
from jax.experimental import pallas as pl
from jax.experimental.pallas import tpu as pltpu
from jax.sharding import PartitionSpec as P

F32 = jnp.float32
BF16 = jnp.bfloat16
BLOCKS = 32
ROWS = 128
OWN = 8
GROUPS = 16
HID = 64
EMB = 32
LENGTH = BLOCKS * ROWS
PADDED = 2 * LENGTH
ROOT_HALF = math.sqrt(0.5)
OUTER = (
    [8 * m for m in range(5)]
    + [4 + 8 * m for m in range(4)]
    + [f + 8 * m for f in (1, 2, 3) for m in range(8)]
)
KEPT = len(OUTER)
PLACE = {k: n for n, k in enumerate(OUTER)}


def dot(a, b, contract=((1,), (0,))):
    return lax.dot_general(a, b, (contract, ((), ())), preferred_element_type=F32)


def halves(x):
    high = x.astype(BF16)
    return high, (x - high.astype(F32)).astype(BF16)


def np_halves(x):
    high = x.astype(ml_dtypes.bfloat16)
    low = (x - high.astype(np.float64)).astype(ml_dtypes.bfloat16)
    return high, low


@functools.cache
def tables():
    t = np.arange(LENGTH, dtype=np.int64)
    e = np.arange(EMB // 2, dtype=np.int64) + 1
    angle = (e[:, None] * t[None, :] % LENGTH).astype(np.float64) * (2 * math.pi / LENGTH)
    high, low = np_halves(np.concatenate([np.sin(angle), np.cos(angle)], axis=0))
    feats = np.concatenate([high, low, high], axis=0)
    n = np.arange(ROWS, dtype=np.int64)
    angle = (n[:, None] * n[None, :] % ROWS).astype(np.float64) * (2 * math.pi / ROWS)
    cos, sin = np.cos(angle), np.sin(angle)
    forward = np.block([[cos, -sin], [sin, cos]])
    back = np.block([[cos, sin], [-sin, cos]]) * (2.0 / PADDED)
    inner = np.stack([*np_halves(forward), *np_halves(back)])
    outer = np.array(OUTER, dtype=np.int64)
    angle = (outer[:, None] * n[None, :]).astype(np.float64) * (2 * math.pi / PADDED)
    turn = np.stack([np.cos(angle), np.sin(angle)]).astype(np.float32)
    turn = np.ascontiguousarray(np.broadcast_to(turn[:, :, None, :], (2, KEPT, OWN, ROWS)))
    return feats, inner, turn


HALF_TURN = (3.140625, 9.67025756835937500e-4, 6.2771141529083251953e-7, 1.2154201256553420e-10)
SIN_SERIES = (1.0, -1 / 6, 1 / 120, -1 / 5040, 1 / 362880, -1 / 39916800)
COS_SERIES = (1.0, -1 / 2, 1 / 24, -1 / 720, 1 / 40320, -1 / 3628800, 1 / 479001600)


def series(coefs, x):
    total = jnp.full_like(x, coefs[-1])
    for coef in coefs[-2::-1]:
        total = total * x + coef
    return total


def sine_cosine(x):
    turns = jnp.round(x * (1 / math.pi))
    rest = x
    for part in HALF_TURN[:3]:
        rest = rest - turns * part
    half = turns * 0.5
    sign = 1.0 - 4.0 * jnp.abs(half - jnp.round(half))
    square = rest * rest
    return sign * rest * series(SIN_SERIES, square), sign * series(COS_SERIES, square)


def c_add(a, b):
    return tuple(p if q is None else q if p is None else p + q for p, q in zip(a, b))


def c_neg(a):
    return tuple(None if p is None else -p for p in a)


def c_sub(a, b):
    return tuple(
        p if q is None else -q if p is None else p - q for p, q in zip(a, b)
    )


def c_turn(a, number, count):
    number = number % count
    if number == 0:
        return a
    if 2 * number == count:
        return c_neg(a)
    re, im = a
    if 4 * number == count:
        return (None if im is None else -im, re)
    if 4 * number == 3 * count:
        return (im, None if re is None else -re)
    cos, sin = math.cos(2 * math.pi * number / count), math.sin(2 * math.pi * number / count)
    if im is None:
        return (re * cos, re * sin)
    if 8 * number == count:
        return ((re - im) * ROOT_HALF, (re + im) * ROOT_HALF)
    if 8 * number == 7 * count:
        return ((re + im) * ROOT_HALF, (im - re) * ROOT_HALF)
    if 8 * number == 3 * count:
        return ((re + im) * -ROOT_HALF, (re - im) * ROOT_HALF)
    if 8 * number == 5 * count:
        return ((im - re) * ROOT_HALF, (re + im) * -ROOT_HALF)
    return (re * cos - im * sin, re * sin + im * cos)


def transform(values, sign):
    count = len(values)
    if count == 1:
        return list(values)
    even, odd = transform(values[::2], sign), transform(values[1::2], sign)
    odd = [c_turn(v, sign * k, count) for k, v in enumerate(odd)]
    return [c_add(a, b) for a, b in zip(even, odd)] + [c_sub(a, b) for a, b in zip(even, odd)]


def outer_forward(x):
    parts = [[None] * 8 for _ in range(5)]
    for b in range(8):
        x0, x1, x2, x3 = x[b], x[8 + b], x[16 + b], x[24 + b]
        plus, minus, other, differ = x0 + x2, x0 - x2, x1 + x3, x1 - x3
        part, whole = differ * ROOT_HALF, other * ROOT_HALF
        parts[0][b] = (plus + other, None)
        parts[4][b] = (plus - other, None)
        parts[2][b] = (minus, -differ)
        parts[1][b] = (x0 + part, -(x2 + whole))
        parts[3][b] = (x0 - part, x2 - whole)
    found = {}
    for f in range(5):
        turned = [c_turn(v, -b * f, 64) for b, v in enumerate(parts[f])]
        for m, v in enumerate(transform(turned, -1)):
            found[f + 8 * m] = v
    return [found[k] for k in OUTER]


def outer_back(z):
    z = {k: z[n] for n, k in enumerate(OUTER)}
    s = ROOT_HALF
    ends, sides = z[0][0] + z[32][0], z[0][0] - z[32][0]
    (r1, i1), (r2, i2), (r3, i3) = z[8], z[16], z[24]
    one, two = s * ((r1 - i1) - (r3 + i3)), s * ((r3 - i3) - (r1 + i1))
    rsum, idiff = r1 + r3, i3 - i1
    v0 = [
        ends + r2 + rsum,
        sides - i2 + one,
        ends - r2 + idiff,
        sides + i2 + two,
        ends + r2 - rsum,
        sides - i2 - one,
        ends - r2 - idiff,
        sides + i2 - two,
    ]
    quarter = [z[4 + 8 * m] for m in range(4)]
    even = transform(quarter, 1)
    odd = transform([c_turn(v, m, 8) for m, v in enumerate(quarter)], 1)
    v4 = []
    for b in range(8):
        re, im = (odd if b % 2 else even)[b // 2]
        angle = 2 * math.pi * b / 16
        v4.append(re if b == 0 else re * math.cos(angle) - im * math.sin(angle))
    v1, v2, v3 = (
        [c_turn(v, b * f, 64) for b, v in enumerate(transform([z[f + 8 * m] for m in range(8)], 1))]
        for f in (1, 2, 3)
    )
    y = [None] * BLOCKS
    for b in range(8):
        (r1, i1), (r2, i2), (r3, i3) = v1[b], v2[b], v3[b]
        ends, sides = v0[b] + v4[b], v0[b] - v4[b]
        y[b] = ends + r2 + (r1 + r3)
        y[8 + b] = sides - i2 + s * ((r1 - i1) - (r3 + i3))
        y[16 + b] = ends - r2 + (i3 - i1)
        y[24 + b] = sides + i2 + s * ((r3 - i3) - (r1 + i1))
    return y


def spread(load, turn, spec):
    for n, (re, im) in enumerate(outer_forward([load(b) for b in range(BLOCKS)])):
        cos, sin = turn[0, n], turn[1, n]
        spec[n, :, :ROWS] = re * cos if im is None else re * cos + im * sin
        spec[n, :, ROWS:] = -(re * sin) if im is None else im * cos - re * sin


def gather(spec, turn):
    z = []
    for n, k in enumerate(OUTER):
        re, im, cos, sin = spec[n, :, :ROWS], spec[n, :, ROWS:], turn[0, n], turn[1, n]
        re, im = re * cos - im * sin, im * cos + re * sin
        z.append((re * 0.5, im * 0.5) if k in (0, 32) else (re, im))
    return outer_back(z)


def inner_pass(x, high, low):
    x_high, x_low = halves(x)
    return dot(x_high, high) + dot(x_low, high) + dot(x_high, low)


def inner_forward(spec, inner):
    x = spec[...].reshape(KEPT * OWN, 2 * ROWS)
    spec[...] = inner_pass(x, inner[0], inner[1]).reshape(KEPT, OWN, 2 * ROWS)


def inner_back(left, right, spec, inner):
    lr, li = left[:, :, :ROWS], left[:, :, ROWS:]
    rr, ri = right[:, :, :ROWS], right[:, :, ROWS:]
    re = (lr * rr + li * ri).reshape(KEPT * OWN, ROWS)
    im = (li * rr - lr * ri).reshape(KEPT * OWN, ROWS)
    x = jnp.concatenate([re, im], axis=1)
    spec[...] = inner_pass(x, inner[2], inner[3]).reshape(KEPT, OWN, 2 * ROWS)


def kernel(
    u_in, g_in, ew_in, fw_in, rate_in, gain_in, feats_in, inner_in, turn_in,
    sig_out, fgrad_out, egrad_out,
    u, g, ew, fw, rate_row, gain_row, feats, inner, turn,
    send_x, recv_x, own_par, pre, active, slopes, base, filt, decays,
    spec_f, spec_u, spec_g, spec_y, bg, q,
    send_s, recv_s, send_f, recv_f, part1, recv1, part2, recv2, part3, recv3,
    in_sem, send_sem, recv_sem,
):
    me, group = lax.axis_index("seq"), lax.axis_index("ch")
    barrier = pltpu.get_barrier_semaphore()

    def greet(axis, own, count):
        @pl.loop(1, count)
        def _(d):
            pl.semaphore_signal(barrier, inc=1, device_id={axis: lax.rem(own + d, count)})

    greet("seq", me, BLOCKS)
    greet("ch", group, GROUPS)

    pairs = (
        (u_in, u), (g_in, g), (ew_in, ew), (fw_in, fw), (rate_in, rate_row), (gain_in, gain_row),
        (feats_in, feats), (inner_in, inner), (turn_in, turn),
    )
    loads = [pltpu.make_async_copy(a, b, in_sem.at[n]) for n, (a, b) in enumerate(pairs)]
    for load in loads:
        load.start()

    def send(n, axis, own, count, source, target):
        @pl.loop(1, count)
        def _(d):
            peer = lax.rem(own + d, count)
            pltpu.make_async_remote_copy(
                src_ref=source(peer),
                dst_ref=target.at[own],
                send_sem=send_sem.at[n],
                recv_sem=recv_sem.at[n],
                device_id={axis: peer},
            ).start()

    def wait(sem, n, ref, count):
        part = ref.at[pl.ds(0, count)]
        pltpu.make_async_copy(part, part, sem.at[n]).wait()

    loads[0].wait()
    loads[1].wait()
    send_x[...] = jnp.concatenate(
        [x[...].astype(F32).T.reshape(BLOCKS, OWN, ROWS) for x in (u, g)], axis=1
    ).astype(BF16)
    pl.semaphore_wait(barrier, BLOCKS + GROUPS - 2)
    send(0, "seq", me, BLOCKS, lambda peer: send_x.at[peer], recv_x)
    recv_x[pl.ds(me, 1)] = send_x[pl.ds(me, 1)]

    for load in loads[2:]:
        load.wait()
    own_par[:, :HID] = fw[...].T
    own_par[:, HID : HID + 8] = jnp.broadcast_to(rate_row[...], (8, BLOCKS * OWN)).T
    own_par[:, HID + 8 : HID + 16] = jnp.broadcast_to(gain_row[...], (8, BLOCKS * OWN)).T
    par = own_par[pl.ds(pl.multiple_of(me * OWN, OWN), OWN), :]
    weight = par[:, :HID]
    rate = jnp.broadcast_to(par[:, HID : HID + 1], (OWN, ROWS))
    gain = jnp.broadcast_to(par[:, HID + 8 : HID + 9], (OWN, ROWS))
    w_high, w_low = halves(weight)

    e_high, e_low = halves(ew[...].T)
    pre[...] = dot(jnp.concatenate([e_high, e_high, e_low], axis=1), feats[...])

    @pl.loop(0, LENGTH // 256)
    def _(n):
        columns = pl.ds(pl.multiple_of(n * 256, 256), 256)
        sine, cosine = sine_cosine(pre[:, columns])
        high, low = halves(sine)
        active[:HID, columns] = high
        active[HID:, columns] = low
        slopes[:, columns] = cosine

    stacked = jnp.concatenate(
        [
            jnp.concatenate([w_high.astype(F32), w_high.astype(F32)], axis=1),
            jnp.concatenate([w_low.astype(F32), jnp.zeros((OWN, HID), F32)], axis=1),
        ],
        axis=0,
    ).astype(BF16)
    base[...] = dot(stacked, active[...])

    lanes = lax.broadcasted_iota(jnp.int32, (OWN, ROWS), 1)
    for b in range(BLOCKS):
        columns = slice(b * ROWS, (b + 1) * ROWS)
        decay = jnp.exp(-rate * (lanes + b * ROWS).astype(F32) / LENGTH)
        decays[b] = decay
        value = (base[:OWN, columns] + base[OWN:, columns]) * decay
        filt[b] = value.astype(BF16).astype(F32)
    spread(lambda b: filt[b], turn, spec_f)
    inner_forward(spec_f, inner)

    wait(recv_sem, 0, recv_x, BLOCKS - 1)
    spread(lambda b: recv_x[b].astype(F32)[:OWN], turn, spec_u)
    spread(lambda b: recv_x[b].astype(F32)[OWN:], turn, spec_g)
    inner_forward(spec_u, inner)
    inner_forward(spec_g, inner)

    inner_back(spec_g, spec_u, spec_y, inner)
    for b, lag in enumerate(gather(spec_y, turn)):
        bg[:, b * ROWS : (b + 1) * ROWS] = lag * decays[b]
    b_high, b_low = halves(bg[...])
    left = jnp.concatenate([w_high, w_low, w_high], axis=0)
    right = jnp.concatenate([b_high, b_high, b_low], axis=0)
    q_high, q_low = halves(dot(left, right, ((0,), (0,))) * slopes[...])
    q[:HID] = q_high
    q[HID:] = q_low
    parts = dot(feats[: 2 * EMB], q[...], ((1,), (1,)))
    embed = parts[:EMB, :HID] + parts[:EMB, HID:] + parts[EMB:, :HID]
    part1[...] = jnp.concatenate([embed[:GROUPS], embed[GROUPS:]], axis=1).reshape(GROUPS, 1, ROWS)
    send(1, "ch", group, GROUPS, lambda peer: part1.at[peer], recv1)
    recv1[pl.ds(group, 1)] = part1[pl.ds(group, 1)]

    inner_back(spec_g, spec_f, spec_y, inner)
    for b, conv in enumerate(gather(spec_y, turn)):
        send_s[b] = (conv + gain * recv_x[b].astype(F32)[OWN:]).astype(BF16)
    send(2, "seq", me, BLOCKS, lambda peer: send_s.at[peer], recv_s)
    recv_s[pl.ds(me, 1)] = send_s[pl.ds(me, 1)]

    wait(recv_sem, 1, recv1, GROUPS - 1)
    part2[...] = jnp.sum(recv1[...], axis=0, keepdims=True)
    send(3, "seq", me, BLOCKS, lambda peer: part2.at[0], recv2)
    recv2[pl.ds(me, 1)] = part2[...]

    parts = dot(jnp.concatenate([b_high, b_low], axis=0), active[...], ((1,), (1,)))
    fgrad = (parts[:OWN, :HID] + parts[:OWN, HID:] + parts[OWN:, :HID]) * (1.0 / LENGTH)
    send_f[0] = jnp.concatenate([fgrad[: OWN // 2], fgrad[OWN // 2 :]], axis=1)
    send(4, "seq", me, BLOCKS, lambda peer: send_f.at[0], recv_f)
    recv_f[pl.ds(me, 1)] = send_f[...]

    wait(recv_sem, 3, recv2, BLOCKS - 1)
    part3[...] = jnp.sum(recv2[...], axis=0, keepdims=True) * (1.0 / math.sqrt(LENGTH))
    send(5, "ch", group, GROUPS, lambda peer: part3.at[0], recv3)
    recv3[pl.ds(group, 1)] = part3[...]

    wait(recv_sem, 2, recv_s, BLOCKS - 1)
    sig_out[...] = recv_s[...].astype(F32).reshape(BLOCKS * OWN, ROWS).T.astype(BF16)

    wait(recv_sem, 4, recv_f, BLOCKS - 1)
    pieces = recv_f[...]
    fgrad_out[...] = (
        jnp.concatenate([pieces[:, :, :HID], pieces[:, :, HID:]], axis=1).reshape(BLOCKS * OWN, HID).T
    )

    wait(recv_sem, 5, recv3, GROUPS - 1)
    embed = recv3[...].reshape(GROUPS, ROWS)
    egrad_out[:GROUPS] = embed[:, :HID]
    egrad_out[GROUPS:] = embed[:, HID:]

    wait(send_sem, 0, send_x, BLOCKS - 1)
    wait(send_sem, 1, part1, GROUPS - 1)
    wait(send_sem, 2, send_s, BLOCKS - 1)
    wait(send_sem, 3, recv2, BLOCKS - 1)
    wait(send_sem, 4, recv_f, BLOCKS - 1)
    wait(send_sem, 5, recv3, GROUPS - 1)


def local(inputs, out_grad, embed_weight, filter_weight, decay_rate, skip_gain):
    channels = inputs.shape[1]
    feats, inner, turn = tables()
    operands = (
        inputs,
        out_grad,
        embed_weight,
        filter_weight,
        decay_rate.reshape(1, channels),
        skip_gain.reshape(1, channels),
        jnp.asarray(feats),
        jnp.asarray(inner),
        jnp.asarray(turn),
    )
    vmem = pltpu.VMEM
    return pl.pallas_call(
        kernel,
        out_shape=(
            jax.ShapeDtypeStruct((ROWS, channels), BF16),
            jax.ShapeDtypeStruct((HID, channels), F32),
            jax.ShapeDtypeStruct((EMB, HID), F32),
        ),
        in_specs=[pl.BlockSpec(memory_space=pl.ANY)] * len(operands),
        out_specs=[pl.BlockSpec(memory_space=pltpu.VMEM)] * 3,
        scratch_shapes=[vmem(x.shape, x.dtype) for x in operands]
        + [
            vmem((BLOCKS, 2 * OWN, ROWS), BF16),
            vmem((BLOCKS, 2 * OWN, ROWS), BF16),
            vmem((channels, ROWS), F32),
            vmem((HID, LENGTH), F32),
            vmem((2 * HID, LENGTH), BF16),
            vmem((HID, LENGTH), F32),
            vmem((2 * OWN, LENGTH), F32),
            vmem((BLOCKS, OWN, ROWS), F32),
            vmem((BLOCKS, OWN, ROWS), F32),
            vmem((KEPT, OWN, 2 * ROWS), F32),
            vmem((KEPT, OWN, 2 * ROWS), F32),
            vmem((KEPT, OWN, 2 * ROWS), F32),
            vmem((KEPT, OWN, 2 * ROWS), F32),
            vmem((OWN, LENGTH), F32),
            vmem((2 * HID, LENGTH), BF16),
            vmem((BLOCKS, OWN, ROWS), BF16),
            vmem((BLOCKS, OWN, ROWS), BF16),
            vmem((1, OWN // 2, ROWS), F32),
            vmem((BLOCKS, OWN // 2, ROWS), F32),
            vmem((GROUPS, 1, ROWS), F32),
            vmem((GROUPS, 1, ROWS), F32),
            vmem((1, 1, ROWS), F32),
            vmem((BLOCKS, 1, ROWS), F32),
            vmem((1, 1, ROWS), F32),
            vmem((GROUPS, 1, ROWS), F32),
            pltpu.SemaphoreType.DMA((len(operands),)),
            pltpu.SemaphoreType.DMA((6,)),
            pltpu.SemaphoreType.DMA((6,)),
        ],
        compiler_params=pltpu.CompilerParams(
            collective_id=0, has_side_effects=True, vmem_limit_bytes=40 * 1024 * 1024
        ),
        name="hyena_backward",
    )(*operands)


def solution(mesh):
    return jax.shard_map(
        local,
        mesh=mesh,
        in_specs=(P("seq", "ch"), P("seq", "ch"), P(), P(None, "ch"), P("ch"), P("ch")),
        out_specs=(P("seq", "ch"), P(None, "ch"), P()),
        check_vma=False,
    )
```

profile of v0, /device:TPU:1, one launch (start us, length us, event | category | flops | bytes accessed | tf_op | source)
XLA Modules:
  0.0 52.4 jit_solution(1742020961110168417)
XLA Ops:
  0.6 0.0 copy-start.8
  0.6 0.0 copy-start.7
  0.7 0.7 %copy-done.8 = f32[256]{0:T(256)S(1)} copy-done((f32[256]{0:T(256)S(1)}, f32[256]{0:T(256)}, u32[]{:S(2)}) %copy-start.8) | copy-done | bytes 1048
  1.3 0.0 copy-done.7
  1.3 0.0 copy-start
  1.3 1.1 %copy-done = bf16[96,4096]{1,0:T(8,128)(2,1)S(1)} copy-done((bf16[96,4096]{1,0:T(8,128)(2,1)S(1)}, bf16[96,4096]{1,0:T(8,128)(2,1)}, u32[]{:S(2)}) %copy-start) | copy-done | bytes 786456
  2.5 0.0 copy-start.1
  2.5 1.0 %copy-done.1 = bf16[4,256,256]{2,1,0:T(8,128)(2,1)S(1)} copy-done((bf16[4,256,256]{2,1,0:T(8,128)(2,1)S(1)}, bf16[4,256,256]{2,1,0:T(8,128)(2,1)}, u32[]{:S(2)}) %copy-start.1) | copy-done | bytes 524312
  3.5 0.0 copy-start.2
  3.5 1.0 %copy-done.2 = f32[2,33,8,128]{3,2,1,0:T(8,128)S(1)} copy-done((f32[2,33,8,128]{3,2,1,0:T(8,128)S(1)}, f32[2,33,8,128]{3,2,1,0:T(8,128)}, u32[]{:S(2)}) %copy-start.2) | copy-done | bytes 270360
  4.5 0.0 copy-start.3
  4.5 0.8 %copy-done.3 = bf16[128,256]{1,0:T(8,128)(2,1)S(1)} copy-done((bf16[128,256]{1,0:T(8,128)(2,1)S(1)}, bf16[128,256]{1,0:T(8,128)(2,1)}, u32[]{:S(2)}) %copy-start.3) | copy-done | bytes 65560
  5.3 0.0 copy-start.4
  5.3 0.8 %copy-done.4 = bf16[128,256]{1,0:T(8,128)(2,1)S(1)} copy-done((bf16[128,256]{1,0:T(8,128)(2,1)S(1)}, bf16[128,256]{1,0:T(8,128)(2,1)}, u32[]{:S(2)}) %copy-start.4) | copy-done | bytes 65560
  6.1 0.0 copy-start.5
  6.1 0.8 %copy-done.5 = f32[64,256]{1,0:T(8,128)S(1)} copy-done((f32[64,256]{1,0:T(8,128)S(1)}, f32[64,256]{1,0:T(8,128)}, u32[]{:S(2)}) %copy-start.5) | copy-done | bytes 65560
  7.0 0.0 copy-start.6
  7.0 0.7 %copy-done.6 = f32[32,64]{1,0:T(8,128)S(1)} copy-done((f32[32,64]{1,0:T(8,128)S(1)}, f32[32,64]{1,0:T(8,128)}, u32[]{:S(2)}) %copy-start.6) | copy-done | bytes 8216
  7.7 42.9 %hyena_backward.1 = (bf16[128,256]{1,0:T(8,128)(2,1)S(1)}, f32[64,256]{1,0:T(8,128)S(1)}, f32[32,64]{1,0:T(8,128)S(1)}) custom-call(bf16[128,256]{1,0:T(8,128)(2,1)S(1)} %copy-done.3, bf16[128,256]{1,0:T(8,128)(2,1)S(1)} %copy-done.4, f32[32,64]{1,0:T(8,128)S(1)} %copy-done.6, f32[64,256]{1,0:T(8,128)S(1)} %copy-done.5, f32[1,256]{1,0:T(1,128)S(1)} %bitcast.2, ...), custom_call_target="tpu_custom_call" | custom-call | tf_op jit(solution)/shard_map/hyena_backward/pallas_call | solution.py:408
  50.6 0.6 %copy.15 = bf16[128,256]{1,0:T(8,128)(2,1)} copy(bf16[128,256]{1,0:T(8,128)(2,1)S(1)} %get-tuple-element.6) | data formatting | bytes 131072
  51.2 0.6 %copy.16 = f32[64,256]{1,0:T(8,128)} copy(f32[64,256]{1,0:T(8,128)S(1)} %get-tuple-element.7) | data formatting | bytes 131072
  51.8 0.6 %copy.17 = f32[32,64]{1,0:T(8,128)} copy(f32[32,64]{1,0:T(8,128)S(1)} %get-tuple-element.8) | data formatting | bytes 16384
Async XLA Ops:
  0.6 0.7 %copy-start.8 = (f32[256]{0:T(256)S(1)}, f32[256]{0:T(256)}, u32[]{:S(2)}) copy-start(f32[256]{0:T(256)} %param.14) | copy-start | bytes 3076
  0.6 0.7 %copy-start.7 = (f32[256]{0:T(256)S(1)}, f32[256]{0:T(256)}, u32[]{:S(2)}) copy-start(f32[256]{0:T(256)} %param.13) | copy-start | bytes 3076
  1.3 1.1 %copy-start = (bf16[96,4096]{1,0:T(8,128)(2,1)S(1)}, bf16[96,4096]{1,0:T(8,128)(2,1)}, u32[]{:S(2)}) copy-start(bf16[96,4096]{1,0:T(8,128)(2,1)} %constant.6.clone.feats_in) | copy-start | bytes 2359300
  2.5 1.0 %copy-start.1 = (bf16[4,256,256]{2,1,0:T(8,128)(2,1)S(1)}, bf16[4,256,256]{2,1,0:T(8,128)(2,1)}, u32[]{:S(2)}) copy-start(bf16[4,256,256]{2,1,0:T(8,128)(2,1)} %constant.7.clone.inner_in) | copy-start | bytes 1572868
  3.5 1.0 %copy-start.2 = (f32[2,33,8,128]{3,2,1,0:T(8,128)S(1)}, f32[2,33,8,128]{3,2,1,0:T(8,128)}, u32[]{:S(2)}) copy-start(f32[2,33,8,128]{3,2,1,0:T(8,128)} %constant.8.clone.turn_in) | copy-start | bytes 811012
  4.5 0.8 %copy-start.3 = (bf16[128,256]{1,0:T(8,128)(2,1)S(1)}, bf16[128,256]{1,0:T(8,128)(2,1)}, u32[]{:S(2)}) copy-start(bf16[128,256]{1,0:T(8,128)(2,1)} %u_in.1) | copy-start | bytes 196612
  5.3 0.8 %copy-start.4 = (bf16[128,256]{1,0:T(8,128)(2,1)S(1)}, bf16[128,256]{1,0:T(8,128)(2,1)}, u32[]{:S(2)}) copy-start(bf16[128,256]{1,0:T(8,128)(2,1)} %g_in.1) | copy-start | bytes 196612
  6.1 0.8 %copy-start.5 = (f32[64,256]{1,0:T(8,128)S(1)}, f32[64,256]{1,0:T(8,128)}, u32[]{:S(2)}) copy-start(f32[64,256]{1,0:T(8,128)} %fw_in.1) | copy-start | bytes 196612
  7.0 0.7 %copy-start.6 = (f32[32,64]{1,0:T(8,128)S(1)}, f32[32,64]{1,0:T(8,128)}, u32[]{:S(2)}) copy-start(f32[32,64]{1,0:T(8,128)} %ew_in.1) | copy-start | bytes 24580
where the time goes:
time: 52.9 us; the launch traced here: 52.4 us
  Pallas kernels  42.9 us (81%)
  local copies, waits for them, and re-layouts  8.9 us (17%)
  between operations  0.67 us (1%)
    pallas_call x1, Pallas kernels, local(): pl.pallas_call(kernel, out_shape=(jax.ShapeDtypeStruct((ROWS, channels),...  42.9 us
    unnamed x21, local copies, waits for them, and re-layouts  8.9 us

commit v1 on v0

--- a/solution.py
+++ b/solution.py
@@ -15,7 +15,10 @@
 BLOCKS = 32
 ROWS = 128
 OWN = 8
-GROUPS = 16
+RUN = 4
+CORES = 2
+PLACES = 8
+RING = 8
 HID = 64
 EMB = 32
 LENGTH = BLOCKS * ROWS
@@ -236,19 +239,54 @@
     u, g, ew, fw, rate_row, gain_row, feats, inner, turn,
     send_x, recv_x, own_par, pre, active, slopes, base, filt, decays,
     spec_f, spec_u, spec_g, spec_y, bg, q,
-    send_s, recv_s, send_f, recv_f, part1, recv1, part2, recv2, part3, recv3,
-    in_sem, send_sem, recv_sem,
+    send_s, recv_s, send_f, recv_f, part1, recv1, part2, recv2,
+    in_sem, send_sem, recv_sem, ready,
 ):
     me, group = lax.axis_index("seq"), lax.axis_index("ch")
+    core, y_low, x = lax.rem(me, CORES), lax.rem(lax.div(me, CORES), RUN), lax.div(me, CORES * RUN)
+    z, y_high = lax.rem(group, RING), lax.div(group, RING)
+    y, place = y_high * RUN + y_low, x * CORES + core
+
+    steps = (4, 5, 3, 6, 2, 7, 1, 0)
+    there = {n: lax.rem(place + n, PLACES) for n in steps}
+    first = {n: lax.div(p, CORES) * (CORES * RUN) + lax.rem(p, CORES) for n, p in there.items()}
+
+    def other_blocks(body):
+        rows = (RUN - 1 - y_low, lax.rem(y_low + 2, RUN), y_low + 1 - 2 * lax.rem(y_low, 2), y_low)
+        for number, row in enumerate(rows):
+            for n in steps:
+                if n or number < RUN - 1:
+                    seq = first[n] + CORES * row
+                    body(seq, {"seq": seq})
+
+    def others_along(own, order, device_of, body):
+        for index in order:
+            for n in steps[:-1]:
+                body(there[n], device_of(n, index))
+
+            @pl.when(own != index)
+            def _():
+                body(place, device_of(0, index))
+
+    def other_y(body):
+        def device(n, index):
+            return {"seq": first[n] + CORES * (index % RUN), "ch": index // RUN * RING + z}
+
+        others_along(y, (0, 1, 7, 2, 6, 3, 5, 4), device, body)
+
+    def other_z(body):
+        def device(n, index):
+            return {"seq": first[n] + CORES * y_low, "ch": y_high * RING + index}
+
+        others_along(z, range(RING), device, body)
+
     barrier = pltpu.get_barrier_semaphore()
-
-    def greet(axis, own, count):
-        @pl.loop(1, count)
-        def _(d):
-            pl.semaphore_signal(barrier, inc=1, device_id={axis: lax.rem(own + d, count)})
-
-    greet("seq", me, BLOCKS)
-    greet("ch", group, GROUPS)
+    relays = [{"ch": (1 - y_high) * RING + z}]
+    relays += [{"ch": y_high * RING + lax.rem(z + n, RING)} for n in (4, 3, 5, 2, 6, 1, 7)]
+
+    other_blocks(lambda _, device: pl.semaphore_signal(barrier, inc=1, device_id=device))
+    for device in relays:
+        pl.semaphore_signal(barrier, inc=1, device_id=device)
 
     pairs = (
         (u_in, u), (g_in, g), (ew_in, ew), (fw_in, fw), (rate_in, rate_row), (gain_in, gain_row),
@@ -258,17 +296,17 @@
     for load in loads:
         load.start()
 
-    def send(n, axis, own, count, source, target):
-        @pl.loop(1, count)
-        def _(d):
-            peer = lax.rem(own + d, count)
+    def send(n, others, own, source, target):
+        def one(there, device):
             pltpu.make_async_remote_copy(
-                src_ref=source(peer),
+                src_ref=source(there),
                 dst_ref=target.at[own],
                 send_sem=send_sem.at[n],
                 recv_sem=recv_sem.at[n],
-                device_id={axis: peer},
+                device_id=device,
             ).start()
+
+        others(one)
 
     def wait(sem, n, ref, count):
         part = ref.at[pl.ds(0, count)]
@@ -279,9 +317,11 @@
     send_x[...] = jnp.concatenate(
         [x[...].astype(F32).T.reshape(BLOCKS, OWN, ROWS) for x in (u, g)], axis=1
     ).astype(BF16)
-    pl.semaphore_wait(barrier, BLOCKS + GROUPS - 2)
-    send(0, "seq", me, BLOCKS, lambda peer: send_x.at[peer], recv_x)
+    pl.semaphore_wait(barrier, BLOCKS - 1 + len(relays))
+    send(0, other_blocks, me, lambda there: send_x.at[there], recv_x)
     recv_x[pl.ds(me, 1)] = send_x[pl.ds(me, 1)]
+    for device in relays:
+        pl.semaphore_signal(ready, inc=1, device_id=device)
 
     for load in loads[2:]:
         load.wait()
@@ -342,31 +382,31 @@
     q[HID:] = q_low
     parts = dot(feats[: 2 * EMB], q[...], ((1,), (1,)))
     embed = parts[:EMB, :HID] + parts[:EMB, HID:] + parts[EMB:, :HID]
-    part1[...] = jnp.concatenate([embed[:GROUPS], embed[GROUPS:]], axis=1).reshape(GROUPS, 1, ROWS)
-    send(1, "ch", group, GROUPS, lambda peer: part1.at[peer], recv1)
-    recv1[pl.ds(group, 1)] = part1[pl.ds(group, 1)]
+    packed = jnp.concatenate([embed[: EMB // 2], embed[EMB // 2 :]], axis=1)
+    for n in range(PLACES):
+        part1[n] = packed[2 * n : 2 * n + 2]
+    pl.semaphore_wait(ready, len(relays))
+    slot = y * PLACES + place
+    send(1, other_y, slot, lambda there: part1.at[there], recv1)
+    recv1[pl.ds(slot, 1)] = part1[pl.ds(place, 1)]
 
     inner_back(spec_g, spec_f, spec_y, inner)
     for b, conv in enumerate(gather(spec_y, turn)):
         send_s[b] = (conv + gain * recv_x[b].astype(F32)[OWN:]).astype(BF16)
-    send(2, "seq", me, BLOCKS, lambda peer: send_s.at[peer], recv_s)
+    send(2, other_blocks, me, lambda there: send_s.at[there], recv_s)
     recv_s[pl.ds(me, 1)] = send_s[pl.ds(me, 1)]
-
-    wait(recv_sem, 1, recv1, GROUPS - 1)
-    part2[...] = jnp.sum(recv1[...], axis=0, keepdims=True)
-    send(3, "seq", me, BLOCKS, lambda peer: part2.at[0], recv2)
-    recv2[pl.ds(me, 1)] = part2[...]
 
     parts = dot(jnp.concatenate([b_high, b_low], axis=0), active[...], ((1,), (1,)))
     fgrad = (parts[:OWN, :HID] + parts[:OWN, HID:] + parts[OWN:, :HID]) * (1.0 / LENGTH)
     send_f[0] = jnp.concatenate([fgrad[: OWN // 2], fgrad[OWN // 2 :]], axis=1)
-    send(4, "seq", me, BLOCKS, lambda peer: send_f.at[0], recv_f)
+    send(4, other_blocks, me, lambda there: send_f.at[0], recv_f)
     recv_f[pl.ds(me, 1)] = send_f[...]
 
-    wait(recv_sem, 3, recv2, BLOCKS - 1)
-    part3[...] = jnp.sum(recv2[...], axis=0, keepdims=True) * (1.0 / math.sqrt(LENGTH))
-    send(5, "ch", group, GROUPS, lambda peer: part3.at[0], recv3)
-    recv3[pl.ds(group, 1)] = part3[...]
+    wait(recv_sem, 1, recv1, RING * PLACES - 1)
+    part2[...] = jnp.sum(recv1[...], axis=0, keepdims=True) * (1.0 / math.sqrt(LENGTH))
+    slot = place * RING + z
+    send(3, other_z, slot, lambda there: part2.at[0], recv2)
+    recv2[pl.ds(slot, 1)] = part2[...]
 
     wait(recv_sem, 2, recv_s, BLOCKS - 1)
     sig_out[...] = recv_s[...].astype(F32).reshape(BLOCKS * OWN, ROWS).T.astype(BF16)
@@ -377,17 +417,25 @@
         jnp.concatenate([pieces[:, :, :HID], pieces[:, :, HID:]], axis=1).reshape(BLOCKS * OWN, HID).T
     )
 
-    wait(recv_sem, 5, recv3, GROUPS - 1)
-    embed = recv3[...].reshape(GROUPS, ROWS)
-    egrad_out[:GROUPS] = embed[:, :HID]
-    egrad_out[GROUPS:] = embed[:, HID:]
+    wait(recv_sem, 3, recv2, RING * PLACES - 1)
+    for n in range(PLACES):
+        piece = jnp.sum(recv2[n * RING : (n + 1) * RING], axis=0)
+        egrad_out[2 * n : 2 * n + 2] = piece[:, :HID]
+        egrad_out[EMB // 2 + 2 * n : EMB // 2 + 2 * n + 2] = piece[:, HID:]
 
     wait(send_sem, 0, send_x, BLOCKS - 1)
-    wait(send_sem, 1, part1, GROUPS - 1)
+    wait(send_sem, 1, recv1, RING * PLACES - 1)
     wait(send_sem, 2, send_s, BLOCKS - 1)
-    wait(send_sem, 3, recv2, BLOCKS - 1)
+    wait(send_sem, 3, recv2, RING * PLACES - 1)
     wait(send_sem, 4, recv_f, BLOCKS - 1)
-    wait(send_sem, 5, recv3, GROUPS - 1)
+
+
+def hand_over(*refs):
+    copies = [pltpu.make_async_copy(refs[n], refs[3 + n], refs[6].at[n]) for n in range(3)]
+    for copy in copies:
+        copy.start()
+    for copy in copies:
+        copy.wait()
 
 
 def local(inputs, out_grad, embed_weight, filter_weight, decay_rate, skip_gain):
@@ -405,14 +453,14 @@
         jnp.asarray(turn),
     )
     vmem = pltpu.VMEM
-    return pl.pallas_call(
+    results = pl.pallas_call(
         kernel,
         out_shape=(
-            jax.ShapeDtypeStruct((ROWS, channels), BF16),
-            jax.ShapeDtypeStruct((HID, channels), F32),
-            jax.ShapeDtypeStruct((EMB, HID), F32),
+            pltpu.VMEM((ROWS, channels), BF16),
+            pltpu.VMEM((HID, channels), F32),
+            pltpu.VMEM((EMB, HID), F32),
         ),
-        in_specs=[pl.BlockSpec(memory_space=pl.ANY)] * len(operands),
+        in_specs=[pl.BlockSpec(memory_space=pltpu.HBM)] * len(operands),
         out_specs=[pl.BlockSpec(memory_space=pltpu.VMEM)] * 3,
         scratch_shapes=[vmem(x.shape, x.dtype) for x in operands]
         + [
@@ -435,21 +483,28 @@
             vmem((BLOCKS, OWN, ROWS), BF16),
             vmem((1, OWN // 2, ROWS), F32),
             vmem((BLOCKS, OWN // 2, ROWS), F32),
-            vmem((GROUPS, 1, ROWS), F32),
-            vmem((GROUPS, 1, ROWS), F32),
-            vmem((1, 1, ROWS), F32),
-            vmem((BLOCKS, 1, ROWS), F32),
-            vmem((1, 1, ROWS), F32),
-            vmem((GROUPS, 1, ROWS), F32),
+            vmem((PLACES, 2, ROWS), F32),
+            vmem((RING * PLACES, 2, ROWS), F32),
+            vmem((1, 2, ROWS), F32),
+            vmem((RING * PLACES, 2, ROWS), F32),
             pltpu.SemaphoreType.DMA((len(operands),)),
-            pltpu.SemaphoreType.DMA((6,)),
-            pltpu.SemaphoreType.DMA((6,)),
+            pltpu.SemaphoreType.DMA((5,)),
+            pltpu.SemaphoreType.DMA((5,)),
+            pltpu.SemaphoreType.REGULAR,
         ],
         compiler_params=pltpu.CompilerParams(
             collective_id=0, has_side_effects=True, vmem_limit_bytes=40 * 1024 * 1024
         ),
         name="hyena_backward",
-    )(*operands)
+    )(*(pltpu.with_memory_space_constraint(x, pltpu.HBM) for x in operands))
+    return pl.pallas_call(
+        hand_over,
+        out_shape=[jax.ShapeDtypeStruct(x.shape, x.dtype) for x in results],
+        in_specs=[pl.BlockSpec(memory_space=pltpu.VMEM)] * 3,
+        out_specs=[pl.BlockSpec(memory_space=pl.ANY)] * 3,
+        scratch_shapes=[pltpu.SemaphoreType.DMA((3,))],
+        name="hand_over",
+    )(*(pltpu.with_memory_space_constraint(x, pltpu.VMEM) for x in results))
 
 
 def solution(mesh):

time: 52.9 us -> 35.9 us (0.68)
  local copies, waits for them, and re-layouts: 8.9 us -> 0 us
  Pallas kernels: 42.9 us -> 35.2 us
    unnamed x21 -> x0, local copies, waits for them, and re-layouts: 8.9 us -> none
    pallas_call x1 -> x2, Pallas kernels: 42.9 us -> 35.2 us  [the longest x1 34.5 us: local(): pl.pallas_call(kernel, out_shape=(pltpu.VMEM((ROWS, channels), BF16), plt...]
where the time goes in v1:
time: 35.9 us; the launch traced here: 35.8 us
  Pallas kernels  35.2 us (98%)
  between operations  0.64 us (2%)
    pallas_call x1, Pallas kernels, local(): pl.pallas_call(kernel, out_shape=(pltpu.VMEM((ROWS, channels), BF16), plt...  34.5 us

profile of v1, /device:TPU:1, one launch (start us, length us, event | category | flops | bytes accessed | tf_op | source)
XLA Modules:
  0.0 35.8 jit_solution(458373226525932083)
XLA Ops:
  0.6 34.5 %hyena_backward.1 = (bf16[128,256]{1,0:T(8,128)(2,1)S(1)}, f32[64,256]{1,0:T(8,128)S(1)}, f32[32,64]{1,0:T(8,128)S(1)}) custom-call(bf16[128,256]{1,0:T(8,128)(2,1)} %u_in.1, bf16[128,256]{1,0:T(8,128)(2,1)} %g_in.1, f32[32,64]{1,0:T(8,128)} %ew_in.1, f32[64,256]{1,0:T(8,128)} %fw_in.1, f32[1,256]{1,0:T(1,128)} %bitcast.2, f32[1,256]{1,0:T(1,128)} %bitcast.3, ...), custom_call_target="tpu_custom_call" | custom-call | tf_op jit(solution)/shard_map/hyena_backward/pallas_call | solution.py:456
  35.1 0.7 %hand_over.1 = (bf16[128,256]{1,0:T(8,128)(2,1)}, f32[64,256]{1,0:T(8,128)}, f32[32,64]{1,0:T(8,128)}) custom-call(bf16[128,256]{1,0:T(8,128)(2,1)S(1)} %get-tuple-element.6.refs_0_, f32[64,256]{1,0:T(8,128)S(1)} %get-tuple-element.7.refs_1_, f32[32,64]{1,0:T(8,128)S(1)} %get-tuple-element.8.refs_2_), custom_call_target="tpu_custom_call" | custom-call | tf_op jit(solution)/shard_map/hand_over/pallas_call | solution.py:500

commit v2 on v1

--- a/solution.py
+++ b/solution.py
@@ -42,6 +42,13 @@
     return high, (x - high.astype(F32)).astype(BF16)
 
 
+def fold(x):
+    while x.shape[0] > 1:
+        half = x.shape[0] // 2
+        x = x[:half] + x[half:]
+    return x
+
+
 def np_halves(x):
     high = x.astype(ml_dtypes.bfloat16)
     low = (x - high.astype(np.float64)).astype(ml_dtypes.bfloat16)
@@ -55,6 +62,7 @@
     angle = (e[:, None] * t[None, :] % LENGTH).astype(np.float64) * (2 * math.pi / LENGTH)
     high, low = np_halves(np.concatenate([np.sin(angle), np.cos(angle)], axis=0))
     feats = np.concatenate([high, low, high], axis=0)
+    columns = np.ascontiguousarray(np.concatenate([high, low], axis=0).T)
     n = np.arange(ROWS, dtype=np.int64)
     angle = (n[:, None] * n[None, :] % ROWS).astype(np.float64) * (2 * math.pi / ROWS)
     cos, sin = np.cos(angle), np.sin(angle)
@@ -65,7 +73,7 @@
     angle = (outer[:, None] * n[None, :]).astype(np.float64) * (2 * math.pi / PADDED)
     turn = np.stack([np.cos(angle), np.sin(angle)]).astype(np.float32)
     turn = np.ascontiguousarray(np.broadcast_to(turn[:, :, None, :], (2, KEPT, OWN, ROWS)))
-    return feats, inner, turn
+    return feats, columns, inner, turn
 
 
 HALF_TURN = (3.140625, 9.67025756835937500e-4, 6.2771141529083251953e-7, 1.2154201256553420e-10)
@@ -234,11 +242,11 @@
 
 
 def kernel(
-    u_in, g_in, ew_in, fw_in, rate_in, gain_in, feats_in, inner_in, turn_in,
+    u_in, g_in, ew_in, fw_in, rate_in, gain_in, feats_in, columns_in, inner_in, turn_in,
     sig_out, fgrad_out, egrad_out,
-    u, g, ew, fw, rate_row, gain_row, feats, inner, turn,
+    u, g, ew, fw, rate_row, gain_row, feats, columns, inner, turn,
     send_x, recv_x, own_par, pre, active, slopes, base, filt, decays,
-    spec_f, spec_u, spec_g, spec_y, bg, q,
+    spec_f, spec_u, spec_g, spec_y, bg, weights,
     send_s, recv_s, send_f, recv_f, part1, recv1, part2, recv2,
     in_sem, send_sem, recv_sem, ready,
 ):
@@ -281,8 +289,12 @@
         others_along(z, range(RING), device, body)
 
     barrier = pltpu.get_barrier_semaphore()
-    relays = [{"ch": (1 - y_high) * RING + z}]
-    relays += [{"ch": y_high * RING + lax.rem(z + n, RING)} for n in (4, 3, 5, 2, 6, 1, 7)]
+
+    def along_z(n):
+        return {"ch": y_high * RING + lax.rem(z + n, RING)}
+
+    second = [along_z(2), along_z(RING - 2)]
+    relays = [{"ch": (1 - y_high) * RING + z}, *second, along_z(1), along_z(RING - 1)]
 
     other_blocks(lambda _, device: pl.semaphore_signal(barrier, inc=1, device_id=device))
     for device in relays:
@@ -290,7 +302,7 @@
 
     pairs = (
         (u_in, u), (g_in, g), (ew_in, ew), (fw_in, fw), (rate_in, rate_row), (gain_in, gain_row),
-        (feats_in, feats), (inner_in, inner), (turn_in, turn),
+        (feats_in, feats), (columns_in, columns), (inner_in, inner), (turn_in, turn),
     )
     loads = [pltpu.make_async_copy(a, b, in_sem.at[n]) for n, (a, b) in enumerate(pairs)]
     for load in loads:
@@ -321,7 +333,7 @@
     send(0, other_blocks, me, lambda there: send_x.at[there], recv_x)
     recv_x[pl.ds(me, 1)] = send_x[pl.ds(me, 1)]
     for device in relays:
-        pl.semaphore_signal(ready, inc=1, device_id=device)
+        pl.semaphore_signal(ready.at[0], inc=1, device_id=device)
 
     for load in loads[2:]:
         load.wait()
@@ -339,12 +351,12 @@
 
     @pl.loop(0, LENGTH // 256)
     def _(n):
-        columns = pl.ds(pl.multiple_of(n * 256, 256), 256)
-        sine, cosine = sine_cosine(pre[:, columns])
+        part = pl.ds(pl.multiple_of(n * 256, 256), 256)
+        sine, cosine = sine_cosine(pre[:, part])
         high, low = halves(sine)
-        active[:HID, columns] = high
-        active[HID:, columns] = low
-        slopes[:, columns] = cosine
+        active[:HID, part] = high
+        active[HID:, part] = low
+        slopes[:, part] = cosine
 
     stacked = jnp.concatenate(
         [
@@ -355,12 +367,16 @@
     ).astype(BF16)
     base[...] = dot(stacked, active[...])
 
+    w_left, w_right = w_high.astype(F32), w_low.astype(F32)
+    tall = jnp.concatenate([w_left, w_left, w_right, jnp.zeros_like(w_left)], axis=0)
+    weights[...] = tall.T.astype(BF16)
+
     lanes = lax.broadcasted_iota(jnp.int32, (OWN, ROWS), 1)
     for b in range(BLOCKS):
-        columns = slice(b * ROWS, (b + 1) * ROWS)
+        part = slice(b * ROWS, (b + 1) * ROWS)
         decay = jnp.exp(-rate * (lanes + b * ROWS).astype(F32) / LENGTH)
         decays[b] = decay
-        value = (base[:OWN, columns] + base[OWN:, columns]) * decay
+        value = (base[:OWN, part] + base[OWN:, part]) * decay
         filt[b] = value.astype(BF16).astype(F32)
     spread(lambda b: filt[b], turn, spec_f)
     inner_forward(spec_f, inner)
@@ -373,22 +389,23 @@
 
     inner_back(spec_g, spec_u, spec_y, inner)
     for b, lag in enumerate(gather(spec_y, turn)):
-        bg[:, b * ROWS : (b + 1) * ROWS] = lag * decays[b]
-    b_high, b_low = halves(bg[...])
-    left = jnp.concatenate([w_high, w_low, w_high], axis=0)
-    right = jnp.concatenate([b_high, b_high, b_low], axis=0)
-    q_high, q_low = halves(dot(left, right, ((0,), (0,))) * slopes[...])
-    q[:HID] = q_high
-    q[HID:] = q_low
-    parts = dot(feats[: 2 * EMB], q[...], ((1,), (1,)))
-    embed = parts[:EMB, :HID] + parts[:EMB, HID:] + parts[EMB:, :HID]
+        grad = lag * decays[b]
+        high = grad.astype(BF16).astype(F32)
+        pair = jnp.concatenate([high, grad - high], axis=0).astype(BF16)
+        bg[: 2 * OWN, b * ROWS : (b + 1) * ROWS] = pair
+        bg[2 * OWN :, b * ROWS : (b + 1) * ROWS] = pair
+    q_high, q_low = halves(dot(weights[...], bg[...]) * slopes[...])
+    parts = dot(jnp.concatenate([q_high, q_low], axis=0), columns[...])
+    embed = (parts[:HID, :EMB] + parts[:HID, EMB:] + parts[HID:, :EMB]).T
     packed = jnp.concatenate([embed[: EMB // 2], embed[EMB // 2 :]], axis=1)
     for n in range(PLACES):
         part1[n] = packed[2 * n : 2 * n + 2]
-    pl.semaphore_wait(ready, len(relays))
+    pl.semaphore_wait(ready.at[0], len(relays))
     slot = y * PLACES + place
     send(1, other_y, slot, lambda there: part1.at[there], recv1)
     recv1[pl.ds(slot, 1)] = part1[pl.ds(place, 1)]
+    for device in second:
+        pl.semaphore_signal(ready.at[1], inc=1, device_id=device)
 
     inner_back(spec_g, spec_f, spec_y, inner)
     for b, conv in enumerate(gather(spec_y, turn)):
@@ -396,15 +413,16 @@
     send(2, other_blocks, me, lambda there: send_s.at[there], recv_s)
     recv_s[pl.ds(me, 1)] = send_s[pl.ds(me, 1)]
 
-    parts = dot(jnp.concatenate([b_high, b_low], axis=0), active[...], ((1,), (1,)))
+    parts = dot(bg[: 2 * OWN], active[...], ((1,), (1,)))
     fgrad = (parts[:OWN, :HID] + parts[:OWN, HID:] + parts[OWN:, :HID]) * (1.0 / LENGTH)
     send_f[0] = jnp.concatenate([fgrad[: OWN // 2], fgrad[OWN // 2 :]], axis=1)
     send(4, other_blocks, me, lambda there: send_f.at[0], recv_f)
     recv_f[pl.ds(me, 1)] = send_f[...]
 
     wait(recv_sem, 1, recv1, RING * PLACES - 1)
-    part2[...] = jnp.sum(recv1[...], axis=0, keepdims=True) * (1.0 / math.sqrt(LENGTH))
+    part2[...] = fold(recv1[...]) * (1.0 / math.sqrt(LENGTH))
     slot = place * RING + z
+    pl.semaphore_wait(ready.at[1], len(second))
     send(3, other_z, slot, lambda there: part2.at[0], recv2)
     recv2[pl.ds(slot, 1)] = part2[...]
 
@@ -417,17 +435,17 @@
         jnp.concatenate([pieces[:, :, :HID], pieces[:, :, HID:]], axis=1).reshape(BLOCKS * OWN, HID).T
     )
 
-    wait(recv_sem, 3, recv2, RING * PLACES - 1)
-    for n in range(PLACES):
-        piece = jnp.sum(recv2[n * RING : (n + 1) * RING], axis=0)
-        egrad_out[2 * n : 2 * n + 2] = piece[:, :HID]
-        egrad_out[EMB // 2 + 2 * n : EMB // 2 + 2 * n + 2] = piece[:, HID:]
-
     wait(send_sem, 0, send_x, BLOCKS - 1)
     wait(send_sem, 1, recv1, RING * PLACES - 1)
     wait(send_sem, 2, send_s, BLOCKS - 1)
     wait(send_sem, 3, recv2, RING * PLACES - 1)
     wait(send_sem, 4, recv_f, BLOCKS - 1)
+
+    wait(recv_sem, 3, recv2, RING * PLACES - 1)
+    for n in range(PLACES):
+        piece = fold(recv2[n * RING : (n + 1) * RING])[0]
+        egrad_out[2 * n : 2 * n + 2] = piece[:, :HID]
+        egrad_out[EMB // 2 + 2 * n : EMB // 2 + 2 * n + 2] = piece[:, HID:]
 
 
 def hand_over(*refs):
@@ -440,7 +458,7 @@
 
 def local(inputs, out_grad, embed_weight, filter_weight, decay_rate, skip_gain):
     channels = inputs.shape[1]
-    feats, inner, turn = tables()
+    feats, columns, inner, turn = tables()
     operands = (
         inputs,
         out_grad,
@@ -449,6 +467,7 @@
         decay_rate.reshape(1, channels),
         skip_gain.reshape(1, channels),
         jnp.asarray(feats),
+        jnp.asarray(columns),
         jnp.asarray(inner),
         jnp.asarray(turn),
     )
@@ -477,8 +496,8 @@
             vmem((KEPT, OWN, 2 * ROWS), F32),
             vmem((KEPT, OWN, 2 * ROWS), F32),
             vmem((KEPT, OWN, 2 * ROWS), F32),
-            vmem((OWN, LENGTH), F32),
-            vmem((2 * HID, LENGTH), BF16),
+            vmem((4 * OWN, LENGTH), BF16),
+            vmem((HID, 4 * OWN), BF16),
             vmem((BLOCKS, OWN, ROWS), BF16),
             vmem((BLOCKS, OWN, ROWS), BF16),
             vmem((1, OWN // 2, ROWS), F32),
@@ -490,7 +509,7 @@
             pltpu.SemaphoreType.DMA((len(operands),)),
             pltpu.SemaphoreType.DMA((5,)),
             pltpu.SemaphoreType.DMA((5,)),
-            pltpu.SemaphoreType.REGULAR,
+            pltpu.SemaphoreType.REGULAR((2,)),
         ],
         compiler_params=pltpu.CompilerParams(
             collective_id=0, has_side_effects=True, vmem_limit_bytes=40 * 1024 * 1024

time: 35.9 us -> 35.6 us (level)
  Pallas kernels: 35.2 us -> 34.8 us
where the time goes in v2:
time: 35.6 us; the launch traced here: 35.5 us
  Pallas kernels  34.8 us (98%)
  between operations  0.64 us (2%)
    pallas_call x1, Pallas kernels, local(): pl.pallas_call(kernel, out_shape=(pltpu.VMEM((ROWS, channels), BF16), plt...  34.1 us

profile of v2, /device:TPU:1, one launch (start us, length us, event | category | flops | bytes accessed | tf_op | source)
XLA Modules:
  0.0 35.5 jit_solution(4508764103339785173)
XLA Ops:
  0.6 34.1 %hyena_backward.1 = (bf16[128,256]{1,0:T(8,128)(2,1)S(1)}, f32[64,256]{1,0:T(8,128)S(1)}, f32[32,64]{1,0:T(8,128)S(1)}) custom-call(bf16[128,256]{1,0:T(8,128)(2,1)} %u_in.1, bf16[128,256]{1,0:T(8,128)(2,1)} %g_in.1, f32[32,64]{1,0:T(8,128)} %ew_in.1, f32[64,256]{1,0:T(8,128)} %fw_in.1, f32[1,256]{1,0:T(1,128)} %bitcast.2, f32[1,256]{1,0:T(1,128)} %bitcast.3, ...), custom_call_target="tpu_custom_call" | custom-call | tf_op jit(solution)/shard_map/hyena_backward/pallas_call | solution.py:475
  34.8 0.7 %hand_over.1 = (bf16[128,256]{1,0:T(8,128)(2,1)}, f32[64,256]{1,0:T(8,128)}, f32[32,64]{1,0:T(8,128)}) custom-call(bf16[128,256]{1,0:T(8,128)(2,1)S(1)} %get-tuple-element.6.refs_0_, f32[64,256]{1,0:T(8,128)S(1)} %get-tuple-element.7.refs_1_, f32[32,64]{1,0:T(8,128)S(1)} %get-tuple-element.8.refs_2_), custom_call_target="tpu_custom_call" | custom-call | tf_op jit(solution)/shard_map/hand_over/pallas_call | solution.py:519

commit v3 on v2

--- a/solution.py
+++ b/solution.py
@@ -245,7 +245,7 @@
     u_in, g_in, ew_in, fw_in, rate_in, gain_in, feats_in, columns_in, inner_in, turn_in,
     sig_out, fgrad_out, egrad_out,
     u, g, ew, fw, rate_row, gain_row, feats, columns, inner, turn,
-    send_x, recv_x, own_par, pre, active, slopes, base, filt, decays,
+    send_u, recv_u, send_g, recv_g, own_par, pre, active, slopes, base, filt, decays,
     spec_f, spec_u, spec_g, spec_y, bg, weights,
     send_s, recv_s, send_f, recv_f, part1, recv1, part2, recv2,
     in_sem, send_sem, recv_sem, ready,
@@ -259,13 +259,14 @@
     there = {n: lax.rem(place + n, PLACES) for n in steps}
     first = {n: lax.div(p, CORES) * (CORES * RUN) + lax.rem(p, CORES) for n, p in there.items()}
 
-    def other_blocks(body):
-        rows = (RUN - 1 - y_low, lax.rem(y_low + 2, RUN), y_low + 1 - 2 * lax.rem(y_low, 2), y_low)
+    def other_blocks(*bodies):
+        rows = [lax.select(y_low == 0, RUN - 1 - n, n + (n >= y_low).astype(jnp.int32)) for n in range(RUN - 1)]
+        rows.append(y_low)
         for number, row in enumerate(rows):
-            for n in steps:
-                if n or number < RUN - 1:
-                    seq = first[n] + CORES * row
-                    body(seq, {"seq": seq})
+            seqs = [first[n] + CORES * row for n in steps if n or number < RUN - 1]
+            for one in bodies:
+                for seq in seqs:
+                    one(seq, {"seq": seq})
 
     def others_along(own, order, device_of, body):
         for index in order:
@@ -309,6 +310,9 @@
         load.start()
 
     def send(n, others, own, source, target):
+        others(sender(n, own, source, target))
+
+    def sender(n, own, source, target):
         def one(there, device):
             pltpu.make_async_remote_copy(
                 src_ref=source(there),
@@ -318,7 +322,7 @@
                 device_id=device,
             ).start()
 
-        others(one)
+        return one
 
     def wait(sem, n, ref, count):
         part = ref.at[pl.ds(0, count)]
@@ -326,12 +330,15 @@
 
     loads[0].wait()
     loads[1].wait()
-    send_x[...] = jnp.concatenate(
-        [x[...].astype(F32).T.reshape(BLOCKS, OWN, ROWS) for x in (u, g)], axis=1
-    ).astype(BF16)
+    for x_ref, send_ref in ((u, send_u), (g, send_g)):
+        send_ref[...] = x_ref[...].astype(F32).T.reshape(BLOCKS, OWN, ROWS).astype(BF16)
     pl.semaphore_wait(barrier, BLOCKS - 1 + len(relays))
-    send(0, other_blocks, me, lambda there: send_x.at[there], recv_x)
-    recv_x[pl.ds(me, 1)] = send_x[pl.ds(me, 1)]
+    other_blocks(
+        sender(0, me, lambda there: send_u.at[there], recv_u),
+        sender(5, me, lambda there: send_g.at[there], recv_g),
+    )
+    recv_u[pl.ds(me, 1)] = send_u[pl.ds(me, 1)]
+    recv_g[pl.ds(me, 1)] = send_g[pl.ds(me, 1)]
     for device in relays:
         pl.semaphore_signal(ready.at[0], inc=1, device_id=device)
 
@@ -381,10 +388,11 @@
     spread(lambda b: filt[b], turn, spec_f)
     inner_forward(spec_f, inner)
 
-    wait(recv_sem, 0, recv_x, BLOCKS - 1)
-    spread(lambda b: recv_x[b].astype(F32)[:OWN], turn, spec_u)
-    spread(lambda b: recv_x[b].astype(F32)[OWN:], turn, spec_g)
+    wait(recv_sem, 0, recv_u, BLOCKS - 1)
+    spread(lambda b: recv_u[b].astype(F32), turn, spec_u)
     inner_forward(spec_u, inner)
+    wait(recv_sem, 5, recv_g, BLOCKS - 1)
+    spread(lambda b: recv_g[b].astype(F32), turn, spec_g)
     inner_forward(spec_g, inner)
 
     inner_back(spec_g, spec_u, spec_y, inner)
@@ -409,7 +417,7 @@
 
     inner_back(spec_g, spec_f, spec_y, inner)
     for b, conv in enumerate(gather(spec_y, turn)):
-        send_s[b] = (conv + gain * recv_x[b].astype(F32)[OWN:]).astype(BF16)
+        send_s[b] = (conv + gain * recv_g[b].astype(F32)).astype(BF16)
     send(2, other_blocks, me, lambda there: send_s.at[there], recv_s)
     recv_s[pl.ds(me, 1)] = send_s[pl.ds(me, 1)]
 
@@ -435,7 +443,8 @@
         jnp.concatenate([pieces[:, :, :HID], pieces[:, :, HID:]], axis=1).reshape(BLOCKS * OWN, HID).T
     )
 
-    wait(send_sem, 0, send_x, BLOCKS - 1)
+    wait(send_sem, 0, send_u, BLOCKS - 1)
+    wait(send_sem, 5, send_g, BLOCKS - 1)
     wait(send_sem, 1, recv1, RING * PLACES - 1)
     wait(send_sem, 2, send_s, BLOCKS - 1)
     wait(send_sem, 3, recv2, RING * PLACES - 1)
@@ -483,8 +492,10 @@
         out_specs=[pl.BlockSpec(memory_space=pltpu.VMEM)] * 3,
         scratch_shapes=[vmem(x.shape, x.dtype) for x in operands]
         + [
-            vmem((BLOCKS, 2 * OWN, ROWS), BF16),
-            vmem((BLOCKS, 2 * OWN, ROWS), BF16),
+            vmem((BLOCKS, OWN, ROWS), BF16),
+            vmem((BLOCKS, OWN, ROWS), BF16),
+            vmem((BLOCKS, OWN, ROWS), BF16),
+            vmem((BLOCKS, OWN, ROWS), BF16),
             vmem((channels, ROWS), F32),
             vmem((HID, LENGTH), F32),
             vmem((2 * HID, LENGTH), BF16),
@@ -507,8 +518,8 @@
             vmem((1, 2, ROWS), F32),
             vmem((RING * PLACES, 2, ROWS), F32),
             pltpu.SemaphoreType.DMA((len(operands),)),
-            pltpu.SemaphoreType.DMA((5,)),
-            pltpu.SemaphoreType.DMA((5,)),
+            pltpu.SemaphoreType.DMA((6,)),
+            pltpu.SemaphoreType.DMA((6,)),
             pltpu.SemaphoreType.REGULAR((2,)),
         ],
         compiler_params=pltpu.CompilerParams(

time: 35.6 us -> 34.8 us (0.978)
  Pallas kernels: 34.8 us -> 34 us
    pallas_call x1, Pallas kernels: 34.1 us -> 33.3 us  [local(): pl.pallas_call(kernel, out_shape=(pltpu.VMEM((ROWS, channels), BF16), plt...]
where the time goes in v3:
time: 34.8 us; the launch traced here: 34.6 us
  Pallas kernels  34 us (98%)
  between operations  0.64 us (2%)
    pallas_call x1, Pallas kernels, local(): pl.pallas_call(kernel, out_shape=(pltpu.VMEM((ROWS, channels), BF16), plt...  33.3 us

profile of v3, /device:TPU:1, one launch (start us, length us, event | category | flops | bytes accessed | tf_op | source)
XLA Modules:
  0.0 34.6 jit_solution(9540826674526811567)
XLA Ops:
  0.6 33.3 %hyena_backward.1 = (bf16[128,256]{1,0:T(8,128)(2,1)S(1)}, f32[64,256]{1,0:T(8,128)S(1)}, f32[32,64]{1,0:T(8,128)S(1)}) custom-call(bf16[128,256]{1,0:T(8,128)(2,1)} %u_in.1, bf16[128,256]{1,0:T(8,128)(2,1)} %g_in.1, f32[32,64]{1,0:T(8,128)} %ew_in.1, f32[64,256]{1,0:T(8,128)} %fw_in.1, f32[1,256]{1,0:T(1,128)} %bitcast.2, f32[1,256]{1,0:T(1,128)} %bitcast.3, ...), custom_call_target="tpu_custom_call" | custom-call | tf_op jit(solution)/shard_map/hyena_backward/pallas_call | solution.py:484
  34.0 0.7 %hand_over.1 = (bf16[128,256]{1,0:T(8,128)(2,1)}, f32[64,256]{1,0:T(8,128)}, f32[32,64]{1,0:T(8,128)}) custom-call(bf16[128,256]{1,0:T(8,128)(2,1)S(1)} %get-tuple-element.6.refs_0_, f32[64,256]{1,0:T(8,128)S(1)} %get-tuple-element.7.refs_1_, f32[32,64]{1,0:T(8,128)S(1)} %get-tuple-element.8.refs_2_), custom_call_target="tpu_custom_call" | custom-call | tf_op jit(solution)/shard_map/hand_over/pallas_call | solution.py:530

commit v4 on v3

--- a/solution.py
+++ b/solution.py
@@ -158,12 +158,9 @@
         parts[2][b] = (minus, -differ)
         parts[1][b] = (x0 + part, -(x2 + whole))
         parts[3][b] = (x0 - part, x2 - whole)
-    found = {}
-    for f in range(5):
+    for f, count in ((0, 5), (4, 4), (1, 8), (2, 8), (3, 8)):
         turned = [c_turn(v, -b * f, 64) for b, v in enumerate(parts[f])]
-        for m, v in enumerate(transform(turned, -1)):
-            found[f + 8 * m] = v
-    return [found[k] for k in OUTER]
+        yield from transform(turned, -1)[:count]
 
 
 def outer_back(z):
@@ -206,11 +203,15 @@
     return y
 
 
-def spread(load, turn, spec):
+def spectrum(load, turn, inner, spec):
+    done = 0
     for n, (re, im) in enumerate(outer_forward([load(b) for b in range(BLOCKS)])):
         cos, sin = turn[0, n], turn[1, n]
         spec[n, :, :ROWS] = re * cos if im is None else re * cos + im * sin
         spec[n, :, ROWS:] = -(re * sin) if im is None else im * cos - re * sin
+        if n + 1 in (KEPT // 2 + 1, KEPT):
+            inner_forward(spec.at[pl.ds(done, n + 1 - done)], inner)
+            done = n + 1
 
 
 def gather(spec, turn):
@@ -228,8 +229,8 @@
 
 
 def inner_forward(spec, inner):
-    x = spec[...].reshape(KEPT * OWN, 2 * ROWS)
-    spec[...] = inner_pass(x, inner[0], inner[1]).reshape(KEPT, OWN, 2 * ROWS)
+    x = spec[...].reshape(-1, 2 * ROWS)
+    spec[...] = inner_pass(x, inner[0], inner[1]).reshape(-1, OWN, 2 * ROWS)
 
 
 def inner_back(left, right, spec, inner):
@@ -385,15 +386,12 @@
         decays[b] = decay
         value = (base[:OWN, part] + base[OWN:, part]) * decay
         filt[b] = value.astype(BF16).astype(F32)
-    spread(lambda b: filt[b], turn, spec_f)
-    inner_forward(spec_f, inner)
+    spectrum(lambda b: filt[b], turn, inner, spec_f)
 
     wait(recv_sem, 0, recv_u, BLOCKS - 1)
-    spread(lambda b: recv_u[b].astype(F32), turn, spec_u)
-    inner_forward(spec_u, inner)
+    spectrum(lambda b: recv_u[b].astype(F32), turn, inner, spec_u)
     wait(recv_sem, 5, recv_g, BLOCKS - 1)
-    spread(lambda b: recv_g[b].astype(F32), turn, spec_g)
-    inner_forward(spec_g, inner)
+    spectrum(lambda b: recv_g[b].astype(F32), turn, inner, spec_g)
 
     inner_back(spec_g, spec_u, spec_y, inner)
     for b, lag in enumerate(gather(spec_y, turn)):

time: 34.8 us -> 34.9 us (level)
  no operation moved by 1% of the time
where the time goes in v4:
time: 34.9 us; the launch traced here: 34.7 us
  Pallas kernels  34.1 us (98%)
  between operations  0.64 us (2%)
    pallas_call x1, Pallas kernels, local(): pl.pallas_call(kernel, out_shape=(pltpu.VMEM((ROWS, channels), BF16), plt...  33.4 us

profile of v4, /device:TPU:1, one launch (start us, length us, event | category | flops | bytes accessed | tf_op | source)
XLA Modules:
  0.0 34.7 jit_solution(9191906613393521778)
XLA Ops:
  0.6 33.4 %hyena_backward.1 = (bf16[128,256]{1,0:T(8,128)(2,1)S(1)}, f32[64,256]{1,0:T(8,128)S(1)}, f32[32,64]{1,0:T(8,128)S(1)}) custom-call(bf16[128,256]{1,0:T(8,128)(2,1)} %u_in.1, bf16[128,256]{1,0:T(8,128)(2,1)} %g_in.1, f32[32,64]{1,0:T(8,128)} %ew_in.1, f32[64,256]{1,0:T(8,128)} %fw_in.1, f32[1,256]{1,0:T(1,128)} %bitcast.2, f32[1,256]{1,0:T(1,128)} %bitcast.3, ...), custom_call_target="tpu_custom_call" | custom-call | tf_op jit(solution)/shard_map/hyena_backward/pallas_call | solution.py:482
  34.0 0.7 %hand_over.1 = (bf16[128,256]{1,0:T(8,128)(2,1)}, f32[64,256]{1,0:T(8,128)}, f32[32,64]{1,0:T(8,128)}) custom-call(bf16[128,256]{1,0:T(8,128)(2,1)S(1)} %get-tuple-element.6.refs_0_, f32[64,256]{1,0:T(8,128)S(1)} %get-tuple-element.7.refs_1_, f32[32,64]{1,0:T(8,128)S(1)} %get-tuple-element.8.refs_2_), custom_call_target="tpu_custom_call" | custom-call | tf_op jit(solution)/shard_map/hand_over/pallas_call | solution.py:528

commit v5 on v3

--- a/solution.py
+++ b/solution.py
@@ -281,13 +281,13 @@
         def device(n, index):
             return {"seq": first[n] + CORES * (index % RUN), "ch": index // RUN * RING + z}
 
-        others_along(y, (0, 1, 7, 2, 6, 3, 5, 4), device, body)
+        others_along(y, (0, 7, 1, 6, 5, 4, 2, 3), device, body)
 
     def other_z(body):
         def device(n, index):
             return {"seq": first[n] + CORES * y_low, "ch": y_high * RING + index}
 
-        others_along(z, range(RING), device, body)
+        others_along(z, (0, 7, 1, 6, 5, 4, 2, 3), device, body)
 
     barrier = pltpu.get_barrier_semaphore()
 
@@ -403,8 +403,8 @@
         bg[: 2 * OWN, b * ROWS : (b + 1) * ROWS] = pair
         bg[2 * OWN :, b * ROWS : (b + 1) * ROWS] = pair
     q_high, q_low = halves(dot(weights[...], bg[...]) * slopes[...])
-    parts = dot(jnp.concatenate([q_high, q_low], axis=0), columns[...])
-    embed = (parts[:HID, :EMB] + parts[:HID, EMB:] + parts[HID:, :EMB]).T
+    parts, low = dot(q_high, columns[...]), dot(q_low, columns[...])
+    embed = (parts[:, :EMB] + parts[:, EMB:] + low[:, :EMB]).T
     packed = jnp.concatenate([embed[: EMB // 2], embed[EMB // 2 :]], axis=1)
     for n in range(PLACES):
         part1[n] = packed[2 * n : 2 * n + 2]

time: 34.8 us -> 34.8 us (level)
  no operation moved by 1% of the time
where the time goes in v5:
time: 34.8 us; the launch traced here: 34.7 us
  Pallas kernels  34 us (98%)
  between operations  0.64 us (2%)
    pallas_call x1, Pallas kernels, local(): pl.pallas_call(kernel, out_shape=(pltpu.VMEM((ROWS, channels), BF16), plt...  33.4 us

profile of v5, /device:TPU:1, one launch (start us, length us, event | category | flops | bytes accessed | tf_op | source)
XLA Modules:
  0.0 34.7 jit_solution(8380788930047157340)
XLA Ops:
  0.6 33.4 %hyena_backward.1 = (bf16[128,256]{1,0:T(8,128)(2,1)S(1)}, f32[64,256]{1,0:T(8,128)S(1)}, f32[32,64]{1,0:T(8,128)S(1)}) custom-call(bf16[128,256]{1,0:T(8,128)(2,1)} %u_in.1, bf16[128,256]{1,0:T(8,128)(2,1)} %g_in.1, f32[32,64]{1,0:T(8,128)} %ew_in.1, f32[64,256]{1,0:T(8,128)} %fw_in.1, f32[1,256]{1,0:T(1,128)} %bitcast.2, f32[1,256]{1,0:T(1,128)} %bitcast.3, ...), custom_call_target="tpu_custom_call" | custom-call | tf_op jit(solution)/shard_map/hyena_backward/pallas_call | solution.py:484
  34.0 0.7 %hand_over.1 = (bf16[128,256]{1,0:T(8,128)(2,1)}, f32[64,256]{1,0:T(8,128)}, f32[32,64]{1,0:T(8,128)}) custom-call(bf16[128,256]{1,0:T(8,128)(2,1)S(1)} %get-tuple-element.6.refs_0_, f32[64,256]{1,0:T(8,128)S(1)} %get-tuple-element.7.refs_1_, f32[32,64]{1,0:T(8,128)S(1)} %get-tuple-element.8.refs_2_), custom_call_target="tpu_custom_call" | custom-call | tf_op jit(solution)/shard_map/hand_over/pallas_call | solution.py:530
